TPU v7x, 512 devices: a whole 4x8x8 slice. The times are simulated.
512 devices in a mesh: section: 16 (over y, z_hi), dp: 16 (over z_lo, x), cores: 2 (over core).
Axes of the slice: x: 4, y: 8, z: 8 (z_hi: 2, z_lo: 4; z = z_hi * 4 + z_lo), core: 2. Of those that a mesh axis runs over, the one named last changes fastest.
Arguments:
- arrivals: bfloat16 [2, 1536, 2048], P(None, 'dp'), may hold values from -6 to 6
- in_flight: bfloat16 [16, 1536, 2048], P('section', 'dp'), may hold values from -6 to 6
- cotangent: bfloat16 [2, 1536, 2048], P(None, 'dp'), may hold values from -6 to 6
- grad_flight: bfloat16 [16, 1536, 2048], P('section', 'dp'), may hold values from -6 to 6
- stashed: bfloat16 [16, 2, 1536, 2048], P('section', None, 'dp'), may hold values from -6 to 6
- in_weight: bfloat16 [16, 2048, 4096], P('section', 'dp', 'cores'), may hold values from -0.125 to 0.125
- out_weight: bfloat16 [16, 1024, 2048], P('section', 'cores', 'dp'), may hold values from -0.1875 to 0.1875
- forward_blocks: int32 [16, 17], P('dp'), may hold values from 1 to 4, 42 in all within a row
- backward_blocks: int32 [16, 17], P('dp'), may hold values from 1 to 4, 42 in all within a row
- forward_marks: int32 [16, 17, 4, 4], P('dp'), may hold values 0 or 1
- backward_marks: int32 [16, 17, 4, 4], P('dp'), may hold values 0 or 1
Outputs:
- activations: bfloat16 [16, 2, 1536, 2048], P('section', None, ('dp', 'cores'))
- input_grads: bfloat16 [16, 2, 1536, 2048], P('section', None, ('dp', 'cores'))
- weight_grads: float32 [16, 1024, 2048], P('section', 'cores', 'dp')
Inputs may be any that keep to these rules, and one draw needn't show every extreme that they name: `forward_blocks`: in each replica's row the 17 lengths add up to 42 blocks and the longest is 4. `backward_blocks`: in each replica's row the 17 lengths add up to 42 blocks and the longest is 4.
All inputs are finite; a program needn't handle non-finite values. No bound on the sum of `forward_marks` or of `backward_marks` on one device may be relied on, other than what follows from the above.
Results may differ from a plain program's by a relative error of at most 0.03.
Values may be sent and summed in bfloat16 or wider, within the bound.
A program may use at most 64 MiB of HBM per device.

v0:
```python
import jax
import jax.numpy as jnp
from jax import lax
from jax.sharding import PartitionSpec as P

HEAD_DIM = 128
BLOCK = 24
BLOCKS = 4
EPSILON = 1e-06


def from_behind(x, axis, by):
    peers = lax.axis_size(axis)
    pairs = [(i, i + by) for i in range(peers) if 0 <= i + by < peers]
    return lax.ppermute(x, axis, pairs)


def block_keep(live_blocks, block_marks):
    length = BLOCKS * BLOCK
    places = jnp.arange(length, dtype=jnp.int32)
    owners = places // BLOCK
    onehot = (owners[:, None] == jnp.arange(BLOCKS, dtype=jnp.int32)[None, :]).astype(jnp.float32)
    spread = jnp.einsum("ia,rab,jb->rij", onehot, block_marks.astype(jnp.float32), onehot)
    allowed = (owners[:, None] == owners[None, :])[None] | (spread > 0.5)
    causal = (places[:, None] >= places[None, :])[None]
    tokens_live = live_blocks * BLOCK
    living = places[None, :] < tokens_live[:, None]
    keeping = causal & allowed & living[:, :, None] & living[:, None, :]
    return (keeping.astype(jnp.float32), 1.0 / tokens_live.astype(jnp.float32))


def choose_history(block_table, mark_table, history):
    histories = block_table.shape[1]
    matches = jnp.arange(histories, dtype=jnp.int32) == history
    blocks = jnp.sum(jnp.where(matches, block_table[0], 0))
    marked = jnp.sum(jnp.where(matches[:, None, None], mark_table[0], 0), axis=0)
    return block_keep(blocks[None], marked[None])


def norm_rows(values_f):
    return lax.rsqrt(jnp.mean(values_f * values_f, axis=-1, keepdims=True) + EPSILON)


def heads_forward(pre_act, keeping, inverse_count):
    scaling = HEAD_DIM ** (-0.5)
    active = jax.nn.silu(pre_act)
    gate_rows = active[:, :, :, 0]
    value_rows = active[:, :, :, 1].astype(jnp.bfloat16)
    query_rows = active[:, :, :, 2].astype(jnp.bfloat16)
    key_rows = active[:, :, :, 3].astype(jnp.bfloat16)
    scores = (
        jnp.einsum("rigd,rjgd->rgij", query_rows, key_rows, preferred_element_type=jnp.float32)
        * scaling
    )
    weights = keeping[:, None] * inverse_count[:, None, None, None]
    attention = (jax.nn.silu(scores) * weights).astype(jnp.bfloat16)
    mixed = jnp.einsum("rgij,rjgd->rigd", attention, value_rows, preferred_element_type=jnp.float32)
    root_scale = lax.rsqrt(jnp.mean(mixed * mixed, axis=-1, keepdims=True) + EPSILON)
    normed = mixed * root_scale
    gated = (normed * gate_rows).astype(jnp.bfloat16)
    return (
        gated,
        (
            gate_rows,
            value_rows,
            query_rows,
            key_rows,
            scores,
            weights,
            attention,
            root_scale,
            normed,
        ),
    )


def heads_backward(pre_act, saved, upstream):
    gate_rows, value_rows, query_rows, key_rows, scores, weights, attention, root_scale, normed = (
        saved
    )
    scaling = HEAD_DIM ** (-0.5)
    grad_gated = upstream.astype(jnp.float32)
    grad_normed = grad_gated * gate_rows
    grad_gate = grad_gated * normed
    grad_mixed = root_scale * (
        grad_normed - normed * jnp.mean(grad_normed * normed, axis=-1, keepdims=True)
    )
    mixed_low = grad_mixed.astype(jnp.bfloat16)
    grad_attention = jnp.einsum(
        "rigd,rjgd->rgij", mixed_low, value_rows, preferred_element_type=jnp.float32
    )
    grad_value = jnp.einsum(
        "rgij,rigd->rjgd", attention, mixed_low, preferred_element_type=jnp.float32
    )
    sigmoid_s = jax.nn.sigmoid(scores)
    grad_scores = (
        grad_attention * weights * sigmoid_s * (1.0 + scores * (1.0 - sigmoid_s)) * scaling
    ).astype(jnp.bfloat16)
    grad_query = jnp.einsum(
        "rgij,rjgd->rigd", grad_scores, key_rows, preferred_element_type=jnp.float32
    )
    grad_key = jnp.einsum(
        "rgij,rigd->rjgd", grad_scores, query_rows, preferred_element_type=jnp.float32
    )
    grad_active = jnp.stack([grad_gate, grad_value, grad_query, grad_key], axis=3)
    sigmoid_u = jax.nn.sigmoid(pre_act)
    return (grad_active * sigmoid_u * (1.0 + pre_act * (1.0 - sigmoid_u))).astype(jnp.bfloat16)


def per_device(
    arrivals,
    in_flight,
    cotangent,
    grad_flight,
    stashed,
    in_weight,
    out_weight,
    forward_blocks,
    backward_blocks,
    forward_marks,
    backward_marks,
):
    section_no = lax.axis_index("section")
    sections = lax.axis_size("section")
    core_no = lax.axis_index("cores")
    ticks = arrivals.shape[0]
    length = arrivals.shape[1]
    share = length // lax.axis_size("cores")
    row_start = core_no * share
    out_full = lax.all_gather(out_weight[0], "dp", axis=1, tiled=True)
    slab_rows = out_full.shape[0]
    groups = slab_rows // HEAD_DIM
    columns = in_weight.shape[2]
    in_full = None
    in_full = lax.all_gather(in_weight[0], "dp", axis=0, tiled=True)
    received = in_flight[0]
    returned = grad_flight[0]
    ahead_out = []
    back_out = []
    gated_list = []
    upstream_list = []
    for tick_no in range(ticks):
        if tick_no == 0:
            prior = in_flight[0]
            later = grad_flight[0]
        else:
            prior = received
            later = returned
        inputs = jnp.where(section_no == 0, arrivals[tick_no], prior)
        upstream = jnp.where(section_no == sections - 1, cotangent[tick_no], later)
        keep_ahead, count_ahead = choose_history(
            forward_blocks, forward_marks, tick_no - section_no + sections - 1
        )
        keep_back, count_back = choose_history(
            backward_blocks, backward_marks, tick_no + section_no
        )
        floats = inputs.astype(jnp.float32)
        saved_floats = stashed[0, tick_no].astype(jnp.float32)
        root_saved = norm_rows(saved_floats)
        scaled_saved = saved_floats * root_saved
        both_normed = jnp.concatenate(
            [(floats * norm_rows(floats)).astype(jnp.bfloat16), scaled_saved.astype(jnp.bfloat16)],
            axis=0,
        )
        pre_both = jnp.dot(both_normed, in_full, preferred_element_type=jnp.float32)
        pre_ahead = pre_both[:length].reshape(1, length, groups, 4, HEAD_DIM)
        pre_back = pre_both[length:].reshape(1, length, groups, 4, HEAD_DIM)
        gated_ahead, unused = heads_forward(pre_ahead, keep_ahead, count_ahead)
        partial_sum = jnp.dot(
            gated_ahead.reshape(length, slab_rows), out_full, preferred_element_type=jnp.float32
        )
        summed = lax.psum(partial_sum.astype(jnp.bfloat16), "cores").astype(jnp.float32)
        outgoing = (floats + summed).astype(jnp.bfloat16)
        ahead_out.append(lax.dynamic_slice_in_dim(outgoing, row_start, share, 0))
        if tick_no + 1 < ticks:
            received = from_behind(outgoing, "section", 1)
        gated_back, saved = heads_forward(pre_back, keep_back, count_back)
        grad_gated = (
            jnp.einsum("sd,fd->sf", upstream, out_full, preferred_element_type=jnp.float32)
            .astype(jnp.bfloat16)
            .reshape(1, length, groups, HEAD_DIM)
        )
        grad_pre = heads_backward(pre_back, saved, grad_gated).reshape(length, columns)
        grad_normed = jnp.einsum("sf,df->sd", grad_pre, in_full, preferred_element_type=jnp.float32)
        back_part = root_saved * (
            grad_normed
            - scaled_saved * jnp.mean(grad_normed * scaled_saved, axis=-1, keepdims=True)
        )
        back_sum = lax.psum(back_part.astype(jnp.bfloat16), "cores").astype(jnp.float32)
        grad_in = (upstream.astype(jnp.float32) + back_sum).astype(jnp.bfloat16)
        back_out.append(lax.dynamic_slice_in_dim(grad_in, row_start, share, 0))
        gated_list.append(gated_back.reshape(length, slab_rows))
        upstream_list.append(upstream)
        if tick_no + 1 < ticks:
            returned = from_behind(grad_in, "section", -1)
    stacked_gated = jnp.concatenate(gated_list, axis=0)
    stacked_upstream = jnp.concatenate(upstream_list, axis=0)
    product = lax.dot_general(
        stacked_gated,
        stacked_upstream,
        (((0,), (0,)), ((), ())),
        preferred_element_type=jnp.float32,
    )
    scaling = (ticks * length * lax.axis_size("dp")) ** (-0.5)
    grads_sum = (
        lax.psum_scatter(
            product.astype(jnp.bfloat16), "dp", scatter_dimension=1, tiled=True
        ).astype(jnp.float32)
        * scaling
    )
    return (jnp.stack(ahead_out)[None], jnp.stack(back_out)[None], grads_sum[None])


def solution(mesh):
    in_specs = (
        P(None, "dp", None),
        P("section", "dp", None),
        P(None, "dp", None),
        P("section", "dp", None),
        P("section", None, "dp", None),
        P("section", "dp", "cores"),
        P("section", "cores", "dp"),
        P("dp", None),
        P("dp", None),
        P("dp", None, None, None),
        P("dp", None, None, None),
    )
    out_specs = (
        P("section", None, ("dp", "cores"), None),
        P("section", None, ("dp", "cores"), None),
        P("section", "cores", "dp"),
    )
    return jax.shard_map(
        per_device, mesh=mesh, in_specs=in_specs, out_specs=out_specs, check_vma=False
    )
```

profile of v0, /device:TPU:8, one launch (start us, length us, event | category | flops | bytes accessed | tf_op | source)
XLA Modules:
  0.0 493.3 jit_solution(5450123814144851031)
XLA Ops:
  8.7 1.4 fusion.137
  11.6 0.9 fusion.128
  12.5 0.9 fusion.125
  13.4 1.2 fusion.72
  14.6 1.4 fusion.78
  16.0 1.0 fusion.38
  17.1 1.0 fusion.48
  18.4 73.2 %all-gather.7.cloned.1.call-done = bf16[1,512,2048]{2,1,0:T(8,128)(2,1)} async-done(((bf16[1,512,128]{2,1,0:T(8,128)(2,1)}), bf16[1,512,2048]{2,1,0:T(8,128)(2,1)}) %all-gather.7.cloned.1.call-update) | async-done | bytes 2097168 | tf_op jit(solution)/shard_map/all_gather | solution.py:130
  91.6 2.4 fusion.31
  94.0 0.7 reshape.833
  94.7 104.7 %all-gather.5.cloned.1.call-done = bf16[1,2048,2048]{2,1,0:T(8,128)(2,1)} async-done(((bf16[1,128,2048]{2,1,0:T(8,128)(2,1)}), bf16[1,2048,2048]{2,1,0:T(8,128)(2,1)}) %all-gather.5.cloned.1.call-update) | async-done | bytes 8388624 | tf_op jit(solution)/shard_map/all_gather | solution.py:135
  199.4 5.2 %fusion.6 = f32[192,2048]{1,0:T(8,128)S(1)} fusion(bf16[1,2048,2048]{2,1,0:T(8,128)(2,1)} %all-gather.5.cloned.1.call-done, bf16[96,2048]{1,0:T(8,128)(2,1)S(1)} %get-tuple-element.54, bf16[96,2048]{1,0:T(8,128)(2,1)S(1)} %get-tuple-element.55), kind=kOutput, calls=%fused_computation.6 | convolution fusion | flops 1612185600 | bytes 10747904 | tf_op jit(solution)/shard_map/dot_general | solution.py:165
  204.8 1.0 copy-done.9
  207.4 0.8 multiply_convert_fusion.6
  208.6 0.9 convolution_bitcast_fusion.8
  209.5 0.8 convolution_bitcast_fusion.2
  210.4 0.9 convolution_bitcast_fusion.9
  213.5 1.4 pad_maximum_fusion
  215.4 1.2 stack.60
  216.6 6.5 %fusion.68 = (f32[96]{0:T(128)S(1)}, f32[96]{0:T(128)S(1)}, f32[96,2048]{1,0:T(8,128)S(1)}) fusion(f32[96]{0:T(128)S(1)} %add_rsqrt_fusion.6, bf16[1,2,96,2048]{3,2,1,0:T(8,128)(2,1)S(1)} %copy-done.1, bf16[1,2048,2048]{2,1,0:T(8,128)(2,1)} %all-gather.5.cloned.1.call-done, f32[96,2048]{1,0:T(8,128)} %stack.60, f32[192,2048]{1,0:T(8,128)S(1)} %copy-done.10), kind=kOutput, calls=%fused_computation.86 | convolution fusion | flops 808451840 | bytes 11535616 | tf_op jit(solution)/shard_map/sf,df->sd/dot_general | solution.py:184
  223.2 1.1 fusion.64
  225.0 1.2 convolution_convert_fusion.2
  228.6 30.0 %all-reduce.7.cloned.1.call-done = (bf16[96,2048]{1,0:T(8,128)(2,1)}, bf16[96,2048]{1,0:T(8,128)(2,1)}) async-done(((bf16[96,2048]{1,0:T(8,128)(2,1)}, bf16[96,2048]{1,0:T(8,128)(2,1)}), (bf16[96,2048]{1,0:T(8,128)(2,1)}, bf16[96,2048]{1,0:T(8,128)(2,1)})) %all-reduce.7.cloned.1.call-update) | async-done | bytes 786448 | tf_op jit(solution)/shard_map/psum | solution.py:172
  258.6 1.2 fusion.80
  259.8 8.1 %collective-permute-start = (bf16[96,2048]{1,0:T(8,128)(2,1)S(1)}, bf16[96,2048]{1,0:T(8,128)(2,1)S(1)}, u32[]{:S(2)}, u32[]{:S(2)}) collective-permute-start(bf16[96,2048]{1,0:T(8,128)(2,1)S(1)} %fusion.80), channel_id=1, source_target_pairs={{0,32},{32,64},{64,96},{96,128},{128,160},{160,192},{192,224},{224... | collective-permute-start | bytes 1179656 | tf_op jit(solution)/shard_map/ppermute | solution.py:15
  267.9 1.9 add_convert_fusion
  269.8 2.8 collective-permute-start.1
  272.6 26.8 %collective-permute-done = bf16[96,2048]{1,0:T(8,128)(2,1)S(1)} collective-permute-done((bf16[96,2048]{1,0:T(8,128)(2,1)S(1)}, bf16[96,2048]{1,0:T(8,128)(2,1)S(1)}, u32[]{:S(2)}, u32[]{:S(2)}) %collective-permute-start) | collective-permute-done | bytes 393248 | tf_op jit(solution)/shard_map/ppermute | solution.py:15
  299.8 5.2 %fusion.4 = f32[192,2048]{1,0:T(8,128)S(1)} fusion(bf16[1,2048,2048]{2,1,0:T(8,128)(2,1)} %all-gather.5.cloned.1.call-done, bf16[96,2048]{1,0:T(8,128)(2,1)S(1)} %copy-done.21, bf16[96,2048]{1,0:T(8,128)(2,1)S(1)} %multiply_convert_fusion.2), kind=kOutput, calls=%fused_computation.4 | convolution fusion | flops 1612185600 | bytes 10747904 | tf_op jit(solution)/shard_map/dot_general | solution.py:165
  305.0 1.2 copy-done.8
  306.2 1.2 fusion.157
  307.5 2.5 reshape.826
  310.0 2.4 fusion.152
  312.6 0.9 multiply_reduce_fusion.2
  313.5 1.0 bitcast_select_fusion
  315.3 1.5 fusion.28
  316.8 1.0 reshape.834
  317.8 1.9 multiply_convert_fusion.5
  319.7 1.2 fusion.106
  320.9 1.2 fusion.21
  322.1 0.9 convolution_bitcast_fusion.6
  323.0 0.8 convolution_bitcast_fusion
  323.9 1.0 convolution_bitcast_fusion.7
  324.8 2.6 reshape.822
  327.4 2.5 fusion.153
  329.9 2.0 multiply_reduce_fusion.5
  331.9 1.1 fusion.97
  333.7 1.2 pad_maximum_fusion.1
  334.9 1.4 copy.67
  336.3 2.4 stack.67
  338.7 6.8 %fusion.73 = (f32[96]{0:T(128)S(1)}, f32[96,2048]{1,0:T(8,128)S(1)}) fusion(f32[96]{0:T(128)S(1)} %add_rsqrt_fusion.4, bf16[1,2,96,2048]{3,2,1,0:T(8,128)(2,1)} %param.15, bf16[1,2048,2048]{2,1,0:T(8,128)(2,1)} %all-gather.5.cloned.1.call-done, f32[96,2048]{1,0:T(8,128)} %stack.67, f32[192,2048]{1,0:T(8,128)} %copy-done.8), kind=kOutput, calls=%fused_computation.91 | convolution fusion | flops 807862144 | bytes 11141888 | tf_op jit(solution)/shard_map/sf,df->sd/dot_general | solution.py:184
  345.5 1.0 fusion.76
  346.5 1.2 convolution_convert_fusion.1
  347.9 1.7 convolution_convert_fusion
  349.7 2.5 copy.74
  352.3 1.0 copy-done.14
  353.2 0.9 dynamic-slice_bitcast_fusion
  354.2 35.7 %all-reduce.5.cloned.1.call-done = (bf16[96,2048]{1,0:T(8,128)(2,1)}, bf16[96,2048]{1,0:T(8,128)(2,1)}) async-done(((bf16[96,2048]{1,0:T(8,128)(2,1)}, bf16[96,2048]{1,0:T(8,128)(2,1)}), (bf16[96,2048]{1,0:T(8,128)(2,1)}, bf16[96,2048]{1,0:T(8,128)(2,1)})) %all-reduce.5.cloned.1.call-update) | async-done | bytes 786448 | tf_op jit(solution)/shard_map/psum | solution.py:172
  389.9 1.0 fusion.95
  390.9 1.0 fusion.94
  391.8 0.8 maximum_bitcast_fusion
  392.6 0.8 maximum_bitcast_fusion.1
  393.4 91.7 %reduce-scatter.4.cloned.1.call-done = bf16[128,512]{1,0:T(8,128)(2,1)} async-done(((bf16[2048,512]{1,0:T(8,128)(2,1)}), bf16[128,512]{1,0:T(8,128)(2,1)}) %reduce-scatter.4.cloned.1.call-update) | async-done | bytes 131088
  485.1 1.0 copy.75
  (116 shorter events, 11.2 us)
Async XLA Ops:
  7.2 11.0 %copy-start.1 = (bf16[1,2,96,2048]{3,2,1,0:T(8,128)(2,1)S(1)}, bf16[1,2,96,2048]{3,2,1,0:T(8,128)(2,1)}, u32[]{:S(2)}) copy-start(bf16[1,2,96,2048]{3,2,1,0:T(8,128)(2,1)} %param.15) | copy-start | bytes 2359300
  7.2 10.9 %copy-start.24 = (bf16[1,96,2048]{2,1,0:T(8,128)(2,1)S(1)}, bf16[1,96,2048]{2,1,0:T(8,128)(2,1)}, u32[]{:S(2)}) copy-start(bf16[1,96,2048]{2,1,0:T(8,128)(2,1)} %param.14) | copy-start | bytes 1179652
  7.2 10.9 %copy-start.17 = (bf16[2,96,2048]{2,1,0:T(8,128)(2,1)S(1)}, bf16[2,96,2048]{2,1,0:T(8,128)(2,1)}, u32[]{:S(2)}) copy-start(bf16[2,96,2048]{2,1,0:T(8,128)(2,1)} %param.13) | copy-start | bytes 2359300
  7.2 84.4 %all-gather.7.cloned.1.call-start = ((), (), s32[]{:S(2)}) async-start(), calls=%async_computation.2 | async-start | bytes 2228224 | tf_op jit(solution)/shard_map/all_gather | solution.py:130
  7.9 191.5 %all-gather.5.cloned.1.call-start = ((), (), s32[]{:S(2)}) async-start(), calls=%async_computation.1 | async-start | bytes 8912896 | tf_op jit(solution)/shard_map/all_gather | solution.py:135
  8.7 249.9 %all-reduce.7.cloned.1.call-start = ((), (), s32[]{:S(2)}) async-start(), calls=%async_computation.5 | async-start | bytes 1572864 | tf_op jit(solution)/shard_map/psum | solution.py:172
  16.0 78.0 %copy-start.5 = (bf16[1,96,2048]{2,1,0:T(8,128)(2,1)}, bf16[1,96,2048]{2,1,0:T(8,128)(2,1)S(1)}, u32[]{:S(2)}) copy-start(bf16[1,96,2048]{2,1,0:T(8,128)(2,1)S(1)} %get-tuple-element.28) | copy-start | bytes 1179652
  204.6 1.1 copy-start.9
  206.3 0.8 copy-start.30
  206.3 1.1 copy-start.7
  210.4 1.8 copy-start.29
  213.5 3.1 copy-start.10
  223.1 1.9 copy-start
  223.2 1.9 copy-start.19
  224.3 34.3 %copy-start.6 = (bf16[1,96,2048]{2,1,0:T(8,128)(2,1)S(1)}, bf16[1,96,2048]{2,1,0:T(8,128)(2,1)}, u32[]{:S(2)}) copy-start(bf16[1,96,2048]{2,1,0:T(8,128)(2,1)} %copy-done.5) | copy-start | bytes 1179652
  226.3 163.6 %all-reduce.5.cloned.1.call-start = ((), (), s32[]{:S(2)}) async-start(), calls=%async_computation.4 | async-start | bytes 1572864 | tf_op jit(solution)/shard_map/psum | solution.py:172
  228.6 84.0 %copy-start.27 = (f32[96,96]{1,0:T(8,128)}, f32[96,96]{1,0:T(8,128)S(1)}, u32[]{:S(2)}) copy-start(f32[96,96]{1,0:T(8,128)S(1)} %fusion.53) | copy-start | bytes 110596
  258.6 40.8 %copy-start.16 = (bf16[2,96,2048]{2,1,0:T(8,128)(2,1)S(1)}, bf16[2,96,2048]{2,1,0:T(8,128)(2,1)}, u32[]{:S(2)}) copy-start(bf16[2,96,2048]{2,1,0:T(8,128)(2,1)} %param.11) | copy-start | bytes 2359300
  259.8 12.8 %copy-start.13 = (bf16[96,2048]{1,0:T(8,128)(2,1)}, bf16[96,2048]{1,0:T(8,128)(2,1)S(1)}, u32[]{:S(2)}) copy-start(bf16[96,2048]{1,0:T(8,128)(2,1)S(1)} %fusion.80) | copy-start | bytes 1179652
  259.8 40.0 %copy-start.21 = (bf16[96,2048]{1,0:T(8,128)(2,1)S(1)}, bf16[96,2048]{1,0:T(8,128)(2,1)}, u32[]{:S(2)}) copy-start(bf16[96,2048]{1,0:T(8,128)(2,1)} %get-tuple-element.37) | copy-start | bytes 1179652
  259.8 39.6 %collective-permute-start = (bf16[96,2048]{1,0:T(8,128)(2,1)S(1)}, bf16[96,2048]{1,0:T(8,128)(2,1)S(1)}, u32[]{:S(2)}, u32[]{:S(2)}) collective-permute-start(bf16[96,2048]{1,0:T(8,128)(2,1)S(1)} %fusion.80), channel_id=1, source_target_pairs={{0,32},{32,64},{64,96},{96,128},{128,160},{160,192},{192,224},{224... | collective-permute-start | bytes 1179656 | tf_op jit(solution)/shard_map/ppermute | solution.py:15
  269.8 43.7 %collective-permute-start.1 = (bf16[96,2048]{1,0:T(8,128)(2,1)}, bf16[96,2048]{1,0:T(8,128)(2,1)}, u32[]{:S(2)}, u32[]{:S(2)}) collective-permute-start(bf16[96,2048]{1,0:T(8,128)(2,1)} %add_convert_fusion), channel_id=1, source_target_pairs={{32,0},{64,32},{96,64},{128,96},{160,128},{192,160},{224,192},{256... | collective-permute-start | bytes 1179656 | tf_op jit(solution)/shard_map/ppermute | solution.py:15
  305.0 1.2 copy-start.8
  310.0 3.5 copy-start.18
  312.4 1.1 copy-start.11
  312.6 0.9 copy-start.25
  314.6 0.7 copy-start.3
  317.8 4.4 copy-start.12
  317.8 6.1 %copy-start.26 = (f32[4,96,96]{2,1,0:T(8,128)S(1)}, f32[4,96,96]{2,1,0:T(8,128)}, u32[]{:S(2)}) copy-start(f32[4,96,96]{2,1,0:T(8,128)} %copy-done.25) | copy-start | bytes 442372
  317.8 6.1 %copy-start.28 = (f32[96,96]{1,0:T(8,128)S(1)}, f32[96,96]{1,0:T(8,128)}, u32[]{:S(2)}) copy-start(f32[96,96]{1,0:T(8,128)} %copy-done.27) | copy-start | bytes 110596
  327.4 6.3 %copy-start.15 = (f32[1,96,4,1,128]{4,1,2,3,0:T(8,128)S(1)}, f32[1,96,4,1,128]{4,1,2,3,0:T(8,128)}, u32[]{:S(2)}) copy-start(f32[1,96,4,1,128]{4,1,2,3,0:T(8,128)} %get-tuple-element.39) | copy-start | bytes 589828
  338.7 6.8 %copy-start.2 = (bf16[1,2,96,2048]{3,2,1,0:T(8,128)(2,1)S(1)}, bf16[1,2,96,2048]{3,2,1,0:T(8,128)(2,1)}, u32[]{:S(2)}) copy-start(bf16[1,2,96,2048]{3,2,1,0:T(8,128)(2,1)} %param.15) | copy-start | bytes 2359300
  338.7 7.8 %copy-start.20 = (bf16[1,96,4,128]{3,2,1,0:T(4,128)(2,1)S(1)}, bf16[1,96,4,128]{3,2,1,0:T(4,128)(2,1)}, u32[]{:S(2)}) copy-start(bf16[1,96,4,128]{3,2,1,0:T(4,128)(2,1)} %copy.53) | copy-start | bytes 294916
  345.4 2.3 copy-start.22
  346.5 1.4 copy-start.23
  347.7 137.4 %reduce-scatter.4.cloned.1.call-start = ((), (), s32[]{:S(2)}) async-start(), calls=%async_computation.3 | async-start | bytes 2228224
  352.2 1.0 copy-start.14
  352.2 38.6 %copy-start.4 = (bf16[96,2048]{1,0:T(8,128)(2,1)S(1)}, bf16[96,2048]{1,0:T(8,128)(2,1)}, u32[]{:S(2)}) copy-start(bf16[96,2048]{1,0:T(8,128)(2,1)} %copy-done.3) | copy-start | bytes 1179652
Sparse Core Ops, SparseCore 0:
  10.0 81.4 all-gather.6
  93.7 105.7 all-gather.4
  226.4 32.1 all-reduce.6
  347.8 42.0 all-reduce.4
  392.6 92.4 reduce-scatter.3
where the time goes:
time: 494 us; the launch traced here: 493 us
  waiting for transfers between devices  364 us (74%)
  matrix products  45.3 us (9%)
  other arithmetic  30.4 us (6%)
  local copies, waits for them, and re-layouts  25.8 us (5%)
  between operations  17.2 us (3%)
  starting transfers between devices  11.1 us (2%)
    all_gather x1, waiting for transfers between devices, per_device(): in_full = lax.all_gather(in_weight[0], 'dp', axis=0, tiled=True)  105 us
    unnamed x6, waiting for transfers between devices  93.1 us
    all_gather x1, waiting for transfers between devices, per_device(): out_full = lax.all_gather(out_weight[0], 'dp', axis=1, tiled=True)  73.2 us
    psum x2, waiting for transfers between devices, per_device(): lax.psum(partial_sum.astype(jnp.bfloat16), 'cores').astype(jnp.float32)  65.7 us
    ppermute x2, waiting for transfers between devices, from_behind(): return lax.ppermute(x, axis, pairs)  26.8 us
    dot_general x2, matrix products, per_device(): jnp.einsum('sf,df->sd', grad_pre, in_full, preferred_element_type=jnp.flo...  13.3 us
    ppermute x2, starting transfers between devices, from_behind(): return lax.ppermute(x, axis, pairs)  10.9 us
    dot_general x2, matrix products, per_device(): pre_both = jnp.dot(both_normed, in_full, preferred_element_type=jnp.float32)  10.4 us
  transfers between devices with their start and end apart: 7, of which 6 were waited for; matrix products, arithmetic and copies ran while one was open for 7% of the time, Pallas kernels for 0%

commit v1 on v0

--- a/solution.py
+++ b/solution.py
@@ -127,7 +127,9 @@
     length = arrivals.shape[1]
     share = length // lax.axis_size("cores")
     row_start = core_no * share
-    out_full = lax.all_gather(out_weight[0], "dp", axis=1, tiled=True)
+    out_full = jnp.concatenate(
+        lax.all_to_all(jnp.stack([out_weight[0]] * lax.axis_size("dp")), "dp", 0, 0), axis=1
+    )
     slab_rows = out_full.shape[0]
     groups = slab_rows // HEAD_DIM
     columns = in_weight.shape[2]

time: 494 us -> 465 us (0.941)
  waiting for transfers between devices: 364 us -> 313 us
  starting transfers between devices: 11.1 us -> 21.1 us
  local copies, waits for them, and re-layouts: 25.8 us -> 32.8 us
    all_to_all x0 -> x1, waiting for transfers between devices: none -> 118 us  [per_device(): lax.all_to_all(jnp.stack([out_weight[0]] * lax.axis_size('dp')), 'dp', 0, 0)]
    all_gather x1, waiting for transfers between devices: 105 us -> 0.02 us  [per_device(): in_full = lax.all_gather(in_weight[0], 'dp', axis=0, tiled=True)]
    all_gather x1 -> x0, waiting for transfers between devices: 73.2 us -> none  [per_device(): out_full = lax.all_gather(out_weight[0], 'dp', axis=1, tiled=True)]
    psum x2, waiting for transfers between devices: 65.7 us -> 76.1 us  [per_device(): lax.psum(partial_sum.astype(jnp.bfloat16), 'cores').astype(jnp.float32)]
    all_to_all x0 -> x1, starting transfers between devices: none -> 9.97 us  [per_device(): lax.all_to_all(jnp.stack([out_weight[0]] * lax.axis_size('dp')), 'dp', 0, 0)]
    unnamed x6 -> x5, waiting for transfers between devices: 93.1 us -> 92.4 us
  transfers between devices with their start and end apart: 7 -> 7, of which waited for: 6 -> 5; matrix products, arithmetic and copies ran while one was open for 7% -> 8% of each run, Pallas kernels for 0% -> 0%
where the time goes in v1:
time: 465 us; the launch traced here: 464 us
  waiting for transfers between devices  313 us (67%)
  matrix products  45.6 us (10%)
  other arithmetic  34 us (7%)
  local copies, waits for them, and re-layouts  32.8 us (7%)
  starting transfers between devices  21.1 us (5%)
  between operations  17.1 us (4%)
    all_to_all x1, waiting for transfers between devices, per_device(): lax.all_to_all(jnp.stack([out_weight[0]] * lax.axis_size('dp')), 'dp', 0, 0)  118 us
    unnamed x5, waiting for transfers between devices  92.4 us
    psum x2, waiting for transfers between devices, per_device(): lax.psum(partial_sum.astype(jnp.bfloat16), 'cores').astype(jnp.float32)  76.1 us
    ppermute x2, waiting for transfers between devices, from_behind(): return lax.ppermute(x, axis, pairs)  26.8 us
    dot_general x2, matrix products, per_device(): jnp.einsum('sf,df->sd', grad_pre, in_full, preferred_element_type=jnp.flo...  13.2 us
    ppermute x2, starting transfers between devices, from_behind(): return lax.ppermute(x, axis, pairs)  11 us
    dot_general x2, matrix products, per_device(): pre_both = jnp.dot(both_normed, in_full, preferred_element_type=jnp.float32)  10.6 us
    another operation x6, other arithmetic  10.1 us
  transfers between devices with their start and end apart: 7, of which 5 were waited for; matrix products, arithmetic and copies ran while one was open for 8% of the time, Pallas kernels for 0%

profile of v1, /device:TPU:8, one launch (start us, length us, event | category | flops | bytes accessed | tf_op | source)
XLA Modules:
  0.0 463.6 jit_solution(12981092719714051457)
XLA Ops:
  7.9 1.0 copy.52
  8.9 1.6 stack.55
  10.5 10.0 %all-to-all-start = ((bf16[16,512,128]{1,2,0:T(8,128)(2,1)}), bf16[16,512,128]{1,2,0:T(8,128)(2,1)S(1)}, u32[]{:S(2)}, u32[]{:S(2)}) async-start(bf16[16,512,128]{1,2,0:T(8,128)(2,1)} %stack.55), calls=%async_computation | async-start | bytes 4194304 | tf_op jit(solution)/shard_map/all_to_all | solution.py:131
  23.3 2.0 fusion.62
  25.8 1.0 fusion.32
  26.8 1.2 select_bitcast_fusion
  28.0 2.1 fusion.51
  30.1 117.6 %all-to-all-done = bf16[16,512,128]{1,2,0:T(8,128)(2,1)S(1)} async-done(((bf16[16,512,128]{1,2,0:T(8,128)(2,1)}), bf16[16,512,128]{1,2,0:T(8,128)(2,1)S(1)}, u32[]{:S(2)}, u32[]{:S(2)}) %all-to-all-start) | async-done | bytes 2097184 | tf_op jit(solution)/shard_map/all_to_all | solution.py:131
  147.7 1.1 fusion.16
  148.9 1.0 reshape.843
  149.9 5.4 %fusion.6 = f32[192,2048]{1,0:T(8,128)S(1)} fusion(bf16[1,2048,2048]{2,1,0:T(8,128)(2,1)} %all-gather.3.cloned.1.call-done, bf16[96,2048]{1,0:T(8,128)(2,1)} %get-tuple-element.54, bf16[96,2048]{1,0:T(8,128)(2,1)} %get-tuple-element.55), kind=kOutput, calls=%fused_computation.6 | convolution fusion | flops 1612185600 | bytes 10747904 | tf_op jit(solution)/shard_map/dot_general | solution.py:167
  155.4 1.2 copy-done.5
  156.6 1.2 fusion.142
  157.8 2.5 reshape.834
  160.4 1.5 fusion.139
  163.6 0.9 convolution_bitcast_fusion.8
  165.3 0.9 convolution_bitcast_fusion.9
  166.3 2.6 reshape.828
  168.8 2.5 fusion.140
  171.3 2.0 multiply_reduce_fusion.6
  173.3 1.2 fusion.83
  174.6 1.5 convolution_convert_fusion.2
  176.2 1.4 copy.62
  177.6 2.4 stack.64
  179.9 6.8 %fusion.52 = (f32[96]{0:T(128)S(1)}, f32[96]{0:T(128)S(1)}, f32[96,2048]{1,0:T(8,128)S(1)}) fusion(f32[96]{0:T(128)S(1)} %add_rsqrt_fusion.6, bf16[1,2,96,2048]{3,2,1,0:T(8,128)(2,1)S(1)} %copy-done, bf16[1,2048,2048]{2,1,0:T(8,128)(2,1)} %all-gather.3.cloned.1.call-done, f32[96,2048]{1,0:T(8,128)} %stack.64, f32[192,2048]{1,0:T(8,128)} %copy-done.5), kind=kOutput, calls=%fused_computation.80 | convolution fusion | flops 808451840 | bytes 11535488 | tf_op jit(solution)/shard_map/sf,df->sd/dot_general | solution.py:186
  186.8 1.2 fusion.48
  190.2 40.4 %all-reduce.7.cloned.1.call-done = (bf16[96,2048]{1,0:T(8,128)(2,1)}, bf16[96,2048]{1,0:T(8,128)(2,1)}) async-done(((bf16[96,2048]{1,0:T(8,128)(2,1)}, bf16[96,2048]{1,0:T(8,128)(2,1)}), (bf16[96,2048]{1,0:T(8,128)(2,1)}, bf16[96,2048]{1,0:T(8,128)(2,1)})) %all-reduce.7.cloned.1.call-update) | async-done | bytes 786448 | tf_op jit(solution)/shard_map/psum | solution.py:174
  230.6 1.2 fusion.64
  231.9 8.1 %collective-permute-start = (bf16[96,2048]{1,0:T(8,128)(2,1)S(1)}, bf16[96,2048]{1,0:T(8,128)(2,1)S(1)}, u32[]{:S(2)}, u32[]{:S(2)}) collective-permute-start(bf16[96,2048]{1,0:T(8,128)(2,1)S(1)} %fusion.64), channel_id=1, source_target_pairs={{0,32},{32,64},{64,96},{96,128},{128,160},{160,192},{192,224},{224... | collective-permute-start | bytes 1179656 | tf_op jit(solution)/shard_map/ppermute | solution.py:15
  240.0 1.8 add_convert_fusion
  241.9 2.8 collective-permute-start.1
  244.7 26.8 %collective-permute-done = bf16[96,2048]{1,0:T(8,128)(2,1)S(1)} collective-permute-done((bf16[96,2048]{1,0:T(8,128)(2,1)S(1)}, bf16[96,2048]{1,0:T(8,128)(2,1)S(1)}, u32[]{:S(2)}, u32[]{:S(2)}) %collective-permute-start) | collective-permute-done | bytes 393248 | tf_op jit(solution)/shard_map/ppermute | solution.py:15
  271.5 1.2 multiply_reduce_fusion
  272.9 5.2 %fusion.4 = f32[192,2048]{1,0:T(8,128)S(1)} fusion(bf16[1,2048,2048]{2,1,0:T(8,128)(2,1)} %all-gather.3.cloned.1.call-done, bf16[96,2048]{1,0:T(8,128)(2,1)S(1)} %copy-done.17, bf16[96,2048]{1,0:T(8,128)(2,1)S(1)} %multiply_convert_fusion.2), kind=kOutput, calls=%fused_computation.4 | convolution fusion | flops 1612185600 | bytes 10747904 | tf_op jit(solution)/shard_map/dot_general | solution.py:167
  278.1 1.2 copy-done.4
  279.3 1.2 fusion.141
  280.5 2.5 reshape.836
  283.1 2.4 fusion.136
  286.6 1.0 bitcast_select_fusion
  288.4 1.1 fusion.17
  289.5 1.0 reshape.844
  290.6 1.9 multiply_convert_fusion.5
  292.5 1.2 fusion.90
  293.7 1.2 fusion.15
  294.9 0.9 convolution_bitcast_fusion.6
  296.6 1.0 convolution_bitcast_fusion.7
  297.6 2.6 reshape.832
  300.1 2.5 fusion.137
  302.6 2.0 multiply_reduce_fusion.5
  304.7 1.2 fusion.81
  305.9 1.5 convolution_convert_fusion.1
  307.5 1.4 copy.69
  308.9 1.4 stack.71
  310.4 6.5 %fusion.57 = (f32[96]{0:T(128)S(1)}, f32[96,2048]{1,0:T(8,128)S(1)}) fusion(f32[96]{0:T(128)S(1)} %add_rsqrt_fusion.4, bf16[1,2,96,2048]{3,2,1,0:T(8,128)(2,1)S(1)} %copy-done.1, bf16[1,2048,2048]{2,1,0:T(8,128)(2,1)} %all-gather.3.cloned.1.call-done, f32[96,2048]{1,0:T(8,128)S(1)} %stack.71, f32[192,2048]{1,0:T(8,128)} %copy-done.4), kind=kOutput, calls=%fused_computation.85 | convolution fusion | flops 807862144 | bytes 11141888 | tf_op jit(solution)/shard_map/sf,df->sd/dot_general | solution.py:186
  316.9 1.0 fusion.60
  318.2 1.7 convolution_convert_fusion
  319.9 2.5 copy.76
  322.5 1.0 copy-done.9
  323.4 0.9 dynamic-slice_bitcast_fusion
  324.4 35.7 %all-reduce.5.cloned.1.call-done = (bf16[96,2048]{1,0:T(8,128)(2,1)}, bf16[96,2048]{1,0:T(8,128)(2,1)}) async-done(((bf16[96,2048]{1,0:T(8,128)(2,1)}, bf16[96,2048]{1,0:T(8,128)(2,1)}), (bf16[96,2048]{1,0:T(8,128)(2,1)}, bf16[96,2048]{1,0:T(8,128)(2,1)})) %all-reduce.5.cloned.1.call-update) | async-done | bytes 786448 | tf_op jit(solution)/shard_map/psum | solution.py:174
  360.1 1.0 fusion.79
  361.1 1.0 fusion.78
  363.6 91.6 %reduce-scatter.4.cloned.1.call-done = bf16[128,512]{1,0:T(8,128)(2,1)} async-done(((bf16[2048,512]{1,0:T(8,128)(2,1)}), bf16[128,512]{1,0:T(8,128)(2,1)}) %reduce-scatter.4.cloned.1.call-update) | async-done | bytes 131088
  455.3 1.0 copy.77
  (119 shorter events, 11.7 us)
Async XLA Ops:
  7.2 142.7 %all-gather.3.cloned.1.call-start = ((), (), s32[]{:S(2)}) async-start(), calls=%async_computation.2 | async-start | bytes 8912896 | tf_op jit(solution)/shard_map/all_gather | solution.py:137
  10.5 10.1 %copy-start.27 = (s32[1,17]{1,0:T(1,128)S(1)}, s32[1,17]{1,0:T(1,128)}, u32[]{:S(2)}) copy-start(s32[1,17]{1,0:T(1,128)} %param.19) | copy-start | bytes 208
  10.5 10.1 %copy-start.28 = (s32[1,17]{1,0:T(1,128)S(1)}, s32[1,17]{1,0:T(1,128)}, u32[]{:S(2)}) copy-start(s32[1,17]{1,0:T(1,128)} %param.18) | copy-start | bytes 208
  10.5 12.2 %copy-start.25 = (s32[1,17,4,4]{1,3,2,0:T(4,128)S(1)}, s32[1,17,4,4]{1,3,2,0:T(4,128)}, u32[]{:S(2)}) copy-start(s32[1,17,4,4]{1,3,2,0:T(4,128)} %param.20) | copy-start | bytes 3268
  10.5 12.5 %copy-start.26 = (s32[1,17,4,4]{1,3,2,0:T(4,128)S(1)}, s32[1,17,4,4]{1,3,2,0:T(4,128)}, u32[]{:S(2)}) copy-start(s32[1,17,4,4]{1,3,2,0:T(4,128)} %param.21) | copy-start | bytes 3268
  10.5 12.7 %copy-start = (bf16[1,2,96,2048]{3,2,1,0:T(8,128)(2,1)S(1)}, bf16[1,2,96,2048]{3,2,1,0:T(8,128)(2,1)}, u32[]{:S(2)}) copy-start(bf16[1,2,96,2048]{3,2,1,0:T(8,128)(2,1)} %param.15) | copy-start | bytes 2359300
  10.5 12.8 %copy-start.20 = (bf16[1,96,2048]{2,1,0:T(8,128)(2,1)S(1)}, bf16[1,96,2048]{2,1,0:T(8,128)(2,1)}, u32[]{:S(2)}) copy-start(bf16[1,96,2048]{2,1,0:T(8,128)(2,1)} %param.12) | copy-start | bytes 1179652
  10.5 137.2 %all-to-all-start = ((bf16[16,512,128]{1,2,0:T(8,128)(2,1)}), bf16[16,512,128]{1,2,0:T(8,128)(2,1)S(1)}, u32[]{:S(2)}, u32[]{:S(2)}) async-start(bf16[16,512,128]{1,2,0:T(8,128)(2,1)} %stack.55), calls=%async_computation | async-start | bytes 4194304 | tf_op jit(solution)/shard_map/all_to_all | solution.py:131
  20.5 210.1 %all-reduce.7.cloned.1.call-start = ((), (), s32[]{:S(2)}) async-start(), calls=%async_computation.5 | async-start | bytes 1572864 | tf_op jit(solution)/shard_map/psum | solution.py:174
  155.3 1.2 copy-start.5
  160.4 1.7 copy-start.31
  171.3 4.8 %copy-start.11 = (f32[1,96,4,1,128]{4,1,2,3,0:T(8,128)S(1)}, f32[1,96,4,1,128]{4,1,2,3,0:T(8,128)}, u32[]{:S(2)}) copy-start(f32[1,96,4,1,128]{4,1,2,3,0:T(8,128)} %get-tuple-element.40) | copy-start | bytes 589828
  173.3 2.8 copy-start.14
  173.3 2.8 copy-start.15
  173.3 2.8 copy-start.22
  188.0 172.1 %all-reduce.5.cloned.1.call-start = ((), (), s32[]{:S(2)}) async-start(), calls=%async_computation.4 | async-start | bytes 1572864 | tf_op jit(solution)/shard_map/psum | solution.py:174
  190.2 95.5 %copy-start.29 = (f32[96,96]{1,0:T(8,128)}, f32[96,96]{1,0:T(8,128)S(1)}, u32[]{:S(2)}) copy-start(f32[96,96]{1,0:T(8,128)S(1)} %fusion.37) | copy-start | bytes 110596
  231.8 12.8 %copy-start.8 = (bf16[96,2048]{1,0:T(8,128)(2,1)}, bf16[96,2048]{1,0:T(8,128)(2,1)S(1)}, u32[]{:S(2)}) copy-start(bf16[96,2048]{1,0:T(8,128)(2,1)S(1)} %fusion.64) | copy-start | bytes 1179652
  231.8 41.0 %copy-start.17 = (bf16[96,2048]{1,0:T(8,128)(2,1)S(1)}, bf16[96,2048]{1,0:T(8,128)(2,1)}, u32[]{:S(2)}) copy-start(bf16[96,2048]{1,0:T(8,128)(2,1)} %get-tuple-element.37) | copy-start | bytes 1179652
  231.9 39.6 %collective-permute-start = (bf16[96,2048]{1,0:T(8,128)(2,1)S(1)}, bf16[96,2048]{1,0:T(8,128)(2,1)S(1)}, u32[]{:S(2)}, u32[]{:S(2)}) collective-permute-start(bf16[96,2048]{1,0:T(8,128)(2,1)S(1)} %fusion.64), channel_id=1, source_target_pairs={{0,32},{32,64},{64,96},{96,128},{128,160},{160,192},{192,224},{224... | collective-permute-start | bytes 1179656 | tf_op jit(solution)/shard_map/ppermute | solution.py:15
  241.9 44.7 %collective-permute-start.1 = (bf16[96,2048]{1,0:T(8,128)(2,1)}, bf16[96,2048]{1,0:T(8,128)(2,1)}, u32[]{:S(2)}, u32[]{:S(2)}) collective-permute-start(bf16[96,2048]{1,0:T(8,128)(2,1)} %add_convert_fusion), channel_id=1, source_target_pairs={{32,0},{64,32},{96,64},{128,96},{160,128},{192,160},{224,192},{256... | collective-permute-start | bytes 1179656 | tf_op jit(solution)/shard_map/ppermute | solution.py:15
  278.1 1.2 copy-start.4
  283.1 3.5 copy-start.16
  285.5 1.1 copy-start.6
  285.7 0.9 copy-start.23
  287.7 0.7 copy-start.2
  290.5 4.4 copy-start.7
  290.6 6.1 %copy-start.24 = (f32[4,96,96]{2,1,0:T(8,128)S(1)}, f32[4,96,96]{2,1,0:T(8,128)}, u32[]{:S(2)}) copy-start(f32[4,96,96]{2,1,0:T(8,128)} %copy-done.23) | copy-start | bytes 442372
  290.6 6.1 %copy-start.30 = (f32[96,96]{1,0:T(8,128)S(1)}, f32[96,96]{1,0:T(8,128)}, u32[]{:S(2)}) copy-start(f32[96,96]{1,0:T(8,128)} %copy-done.29) | copy-start | bytes 110596
  302.6 4.8 %copy-start.10 = (f32[1,96,4,1,128]{4,1,2,3,0:T(8,128)S(1)}, f32[1,96,4,1,128]{4,1,2,3,0:T(8,128)}, u32[]{:S(2)}) copy-start(f32[1,96,4,1,128]{4,1,2,3,0:T(8,128)} %get-tuple-element.39) | copy-start | bytes 589828
  304.6 2.8 copy-start.12
  304.6 2.8 copy-start.13
  304.6 2.8 copy-start.21
  307.4 2.9 copy-start.1
  316.9 1.1 copy-start.18
  316.9 1.2 copy-start.19
  317.9 137.3 %reduce-scatter.4.cloned.1.call-start = ((), (), s32[]{:S(2)}) async-start(), calls=%async_computation.3 | async-start | bytes 2228224
  322.4 1.0 copy-start.9
  322.4 38.6 %copy-start.3 = (bf16[96,2048]{1,0:T(8,128)(2,1)S(1)}, bf16[96,2048]{1,0:T(8,128)(2,1)}, u32[]{:S(2)}) copy-start(bf16[96,2048]{1,0:T(8,128)(2,1)} %copy-done.2) | copy-start | bytes 1179652
Sparse Core Ops, SparseCore 0:
  10.1 135.6 all-gather.2
  188.1 42.4 all-reduce.6
  318.0 42.0 all-reduce.4
  362.8 92.4 reduce-scatter.3
